TPU v7x, 1024 devices: a whole 8x8x8 slice. The times are simulated.
1024 devices in a mesh: blk: 32 (over x, y_lo, core), dp: 32 (over z, y_hi).
Axes of the slice: x: 8, y: 8 (y_hi: 4, y_lo: 2; y = y_hi * 2 + y_lo), z: 8, core: 2. Of those that a mesh axis runs over, the one named last changes fastest.
Arguments:
- tokens: bfloat16 [8192, 16384], P('dp', 'blk'), may hold values from -6 to 6
- cotangent: bfloat16 [8192, 16384], P('dp', 'blk'), may hold values from -6 to 6
- up_first: bfloat16 [128, 128, 128], P('blk'), may hold values from -0.5 to 0.5
- up_second: bfloat16 [128, 128, 416], P('blk'), may hold values from -0.5 to 0.5
- down_first: bfloat16 [128, 416, 128], P('blk'), may hold values from -0.3125 to 0.3125
- down_second: bfloat16 [128, 128, 128], P('blk'), may hold values from -0.5 to 0.5
Outputs:
- grad_tokens: bfloat16 [8192, 16384], P('dp', 'blk')
- grad_up_first: float32 [128, 128, 128], P('blk', 'dp')
- grad_up_second: float32 [128, 128, 416], P('blk', 'dp')
- grad_down_first: float32 [128, 416, 128], P('blk', 'dp')
- grad_down_second: float32 [128, 128, 128], P('blk', 'dp')
All inputs are finite; a program needn't handle non-finite values.
Results may differ from a plain program's by a relative error of at most 0.03.
Values may be sent and summed in bfloat16 or wider, within the bound.
A program may use at most 32 MiB of HBM per device.

v0:
```python
import jax
import jax.numpy as jnp
from jax import lax
from jax.sharding import PartitionSpec as P


def gelu_tanh(value):
    inner_arg = 0.7978845608 * (value + 0.044715 * value * value * value)
    return 0.5 * value * (1.0 + jnp.tanh(inner_arg))


def gelu_slope(value):
    tangent = jnp.tanh(0.7978845608 * (value + 0.044715 * value * value * value))
    return 0.5 * (1.0 + tangent) + 0.5 * value * (1.0 - tangent * tangent) * 0.7978845608 * (
        1.0 + 3.0 * 0.044715 * value * value
    )


def forward_layout(block_out, blk_count, blk_dev, inner_count, tok_rows):
    return block_out.reshape(blk_count, blk_dev * inner_count, blk_dev, tok_rows)


def inverse_layout(block_in, blk_count, blk_dev, inner_count, tok_rows):
    spread = block_in.reshape(blk_dev, inner_count, blk_count, blk_dev, tok_rows)
    return spread.transpose(2, 3, 0, 1, 4).reshape(
        blk_count, blk_dev, blk_dev, inner_count * tok_rows
    )


def middle_forward(permuted, up_second, down_first):
    pre_act = jnp.einsum("cjt,cjh->tch", permuted, up_second, preferred_element_type=jnp.float32)
    activated = gelu_tanh(pre_act).astype(jnp.bfloat16)
    down_out = jnp.einsum(
        "tbh,bho->obt", activated, down_first, preferred_element_type=jnp.float32
    ).astype(jnp.bfloat16)
    return (pre_act, activated, down_out)


def middle_backward(grad_down, pre_act, up_second, down_first):
    grad_act = jnp.einsum("bot,bho->tbh", grad_down, down_first, preferred_element_type=jnp.float32)
    grad_pre = (grad_act * gelu_slope(pre_act)).astype(jnp.bfloat16)
    grad_perm = jnp.einsum(
        "tch,cjh->cjt", grad_pre, up_second, preferred_element_type=jnp.float32
    ).astype(jnp.bfloat16)
    return (grad_pre, grad_perm)


def body(tokens, cotangent, up_first, up_second, down_first, down_second):
    blk_dev = up_first.shape[0]
    block_size = up_first.shape[1]
    blk_count = lax.axis_size("blk")
    tok_rows = tokens.shape[0]
    inner_count = block_size // (blk_dev * blk_count)
    tok_blocks = tokens.reshape(tok_rows, blk_dev, block_size)
    cot_blocks = cotangent.reshape(tok_rows, blk_dev, block_size)
    first = jnp.einsum(
        "tbi,bio->obt", tok_blocks, up_first, preferred_element_type=jnp.float32
    ).astype(jnp.bfloat16)
    send_first = forward_layout(first, blk_count, blk_dev, inner_count, tok_rows)
    grad_mixed = jnp.einsum(
        "tco,cjo->cjt", cot_blocks, down_second, preferred_element_type=jnp.float32
    ).astype(jnp.bfloat16)
    send_mixed = inverse_layout(grad_mixed, blk_count, blk_dev, inner_count, tok_rows)
    got_first = lax.all_to_all(send_first, "blk", split_axis=0, concat_axis=2, tiled=True)
    permuted = got_first.reshape(blk_dev, block_size, tok_rows)
    pre_act, activated, down_out = middle_forward(permuted, up_second, down_first)
    got_down = lax.all_to_all(
        forward_layout(down_out, blk_count, blk_dev, inner_count, tok_rows),
        "blk",
        split_axis=0,
        concat_axis=2,
        tiled=True,
    )
    got_mixed = lax.all_to_all(send_mixed, "blk", split_axis=0, concat_axis=2, tiled=True)
    grad_down = got_mixed.reshape(blk_dev, block_size, tok_rows)
    grad_pre, grad_perm = middle_backward(grad_down, pre_act, up_second, down_first)
    got_perm = lax.all_to_all(
        inverse_layout(grad_perm, blk_count, blk_dev, inner_count, tok_rows),
        "blk",
        split_axis=0,
        concat_axis=2,
        tiled=True,
    )
    mixed = got_down.reshape(blk_dev, block_size, tok_rows)
    grad_first = got_perm.reshape(blk_dev, block_size, tok_rows)
    grad_out = jnp.einsum(
        "bot,bio->tbi", grad_first, up_first, preferred_element_type=jnp.float32
    ).astype(jnp.bfloat16)
    grad_out = grad_out.reshape(tok_rows, blk_dev * block_size)
    term_up_one = jnp.einsum(
        "tbi,bot->bio", tok_blocks, grad_first, preferred_element_type=jnp.float32
    )
    term_up_two = jnp.einsum("cjt,tch->cjh", permuted, grad_pre, preferred_element_type=jnp.float32)
    term_down_one = jnp.einsum(
        "tbh,bot->bho", activated, grad_down, preferred_element_type=jnp.float32
    )
    term_down_two = jnp.einsum(
        "cjt,tco->cjo", mixed, cot_blocks, preferred_element_type=jnp.float32
    )
    sum_up_one, sum_up_two, sum_down_one, sum_down_two = (
        lax.psum_scatter(
            term_up_one.astype(jnp.bfloat16), "dp", scatter_dimension=1, tiled=True
        ).astype(jnp.float32),
        lax.psum_scatter(
            term_up_two.astype(jnp.bfloat16), "dp", scatter_dimension=1, tiled=True
        ).astype(jnp.float32),
        lax.psum_scatter(
            term_down_one.astype(jnp.bfloat16), "dp", scatter_dimension=1, tiled=True
        ).astype(jnp.float32),
        lax.psum_scatter(
            term_down_two.astype(jnp.bfloat16), "dp", scatter_dimension=1, tiled=True
        ).astype(jnp.float32),
    )
    factor = float(tok_rows * lax.axis_size("dp")) ** (-0.5)
    return (
        grad_out,
        sum_up_one * factor,
        sum_up_two * factor,
        sum_down_one * factor,
        sum_down_two * factor,
    )


def solution(mesh):
    in_specs = (
        P("dp", "blk"),
        P("dp", "blk"),
        P("blk", None, None),
        P("blk", None, None),
        P("blk", None, None),
        P("blk", None, None),
    )
    out_specs = (
        P("dp", "blk"),
        P("blk", "dp", None),
        P("blk", "dp", None),
        P("blk", "dp", None),
        P("blk", "dp", None),
    )
    return jax.shard_map(body, mesh=mesh, in_specs=in_specs, out_specs=out_specs, check_vma=False)
```

profile of v0, /device:TPU:12, one launch (start us, length us, event | category | flops | bytes accessed | tf_op | source)
XLA Modules:
  0.0 431.2 jit_solution(7480972281792808267)
XLA Ops:
  7.2 1.3 fusion.7
  8.6 0.8 copy.30
  9.4 16.7 %all-to-all-start.1 = ((bf16[32,4,4,256]{3,1,2,0:T(4,128)(2,1)}), bf16[32,4,4,256]{3,1,2,0:T(4,128)(2,1)S(1)}, u32[]{:S(2)}, u32[]{:S(2)}) async-start(bf16[32,4,4,256]{3,1,2,0:T(4,128)(2,1)} %copy.30), calls=%async_computation.1 | async-start | bytes 524288 | tf_op jit(solution)/shard_map/all_to_all | solution.py:64
  26.5 0.8 copy.86
  27.3 8.1 %all-to-all-done.1 = bf16[32,4,4,256]{3,1,2,0:T(4,128)(2,1)S(1)} async-done(((bf16[32,4,4,256]{3,1,2,0:T(4,128)(2,1)}), bf16[32,4,4,256]{3,1,2,0:T(4,128)(2,1)S(1)}, u32[]{:S(2)}, u32[]{:S(2)}) %all-to-all-start.1) | async-done | bytes 262176 | tf_op jit(solution)/shard_map/all_to_all | solution.py:64
  35.4 7.0 %all-to-all-start = ((bf16[32,4,4,256]{3,1,2,0:T(4,128)(2,1)}), bf16[32,4,4,256]{3,1,2,0:T(4,128)(2,1)S(1)}, u32[]{:S(2)}, u32[]{:S(2)}) async-start(bf16[32,4,4,256]{3,1,2,0:T(4,128)(2,1)} %bitcast.96), calls=%async_computation | async-start | bytes 524288 | tf_op jit(solution)/shard_map/all_to_all | solution.py:74
  42.8 8.8 %all-to-all-done = bf16[32,4,4,256]{3,1,2,0:T(4,128)(2,1)S(1)} async-done(((bf16[32,4,4,256]{3,1,2,0:T(4,128)(2,1)}), bf16[32,4,4,256]{3,1,2,0:T(4,128)(2,1)S(1)}, u32[]{:S(2)}, u32[]{:S(2)}) %all-to-all-start) | async-done | bytes 262176 | tf_op jit(solution)/shard_map/all_to_all | solution.py:74
  51.6 2.3 fusion.6
  53.9 1.1 fusion.8
  54.9 1.0 reshape.60
  55.9 0.8 copy.85
  56.7 7.0 %all-to-all-start.2 = ((bf16[32,4,4,256]{3,1,2,0:T(4,128)(2,1)}), bf16[32,4,4,256]{3,1,2,0:T(4,128)(2,1)S(1)}, u32[]{:S(2)}, u32[]{:S(2)}) async-start(bf16[32,4,4,256]{3,1,2,0:T(4,128)(2,1)} %bitcast.101), calls=%async_computation.2 | async-start | bytes 524288 | tf_op jit(solution)/shard_map/all_to_all | solution.py:77
  63.8 2.5 fusion.9
  66.2 1.7 reshape.64
  67.9 1.7 copy.37
  69.7 3.3 all-to-all-done.2
  73.0 7.7 %all-to-all-start.3 = ((bf16[32,4,4,256]{3,1,2,0:T(4,128)(2,1)}), bf16[32,4,4,256]{3,1,2,0:T(4,128)(2,1)}, u32[]{:S(2)}, u32[]{:S(2)}) async-start(bf16[32,4,4,256]{3,1,2,0:T(4,128)(2,1)} %copy.37), calls=%async_computation.3 | async-start | bytes 524288 | tf_op jit(solution)/shard_map/all_to_all | solution.py:67
  80.7 1.6 convolution_convert_fusion.1
  82.4 1.0 copy.36
  83.4 1.2 convolution_convert_fusion
  84.8 0.8 copy.35
  85.6 4.3 %all-to-all-done.3 = bf16[32,4,4,256]{3,1,2,0:T(4,128)(2,1)} async-done(((bf16[32,4,4,256]{3,1,2,0:T(4,128)(2,1)}), bf16[32,4,4,256]{3,1,2,0:T(4,128)(2,1)}, u32[]{:S(2)}, u32[]{:S(2)}) %all-to-all-start.3) | async-done | bytes 262176 | tf_op jit(solution)/shard_map/all_to_all | solution.py:67
  89.9 1.2 convolution_convert_fusion.7
  91.1 0.7 copy.40
  91.9 1.3 dynamic-slice
  94.7 0.8 copy.41
  95.5 324.3 %all-reduce.7.cloned.1.call-done = (bf16[4,128,128]{2,0,1:T(4,128)(2,1)}, bf16[4,128,416]{2,1,0:T(8,128)(2,1)}, bf16[4,416,128]{2,0,1:T(4,128)(2,1)}, bf16[4,128,128]{2,0,1:T(4,128)(2,1)}) async-done(((bf16[4,128,128]{2,0,1:T(4,128)(2,1)}, bf16[4,128,416]{2,1,0:T(8,128)(2,1)}, bf16[4,416,128]{2,0,1:T(4,128)(2,1)}, bf16[4,128,128]{2,0,1:T(4,128)(2,1)}), (bf16[4,128,128]{2,0,1:T(4,128)(2,1)}, ...) | async-done | bytes 1114128
  419.8 0.7 convert_multiply_fusion.2
  420.5 0.6 copy.42
  421.1 0.6 copy.43
  421.7 1.4 convert_multiply_fusion
  423.1 1.3 convert_multiply_fusion.1
  (22 shorter events, 1.2 us)
Async XLA Ops:
  7.2 35.2 %copy-start = (bf16[4,128,416]{1,2,0:T(8,128)(2,1)S(1)}, bf16[4,128,416]{1,2,0:T(8,128)(2,1)}, u32[]{:S(2)}) copy-start(bf16[4,128,416]{1,2,0:T(8,128)(2,1)} %param.9) | copy-start | bytes 1277956
  7.2 19.0 %copy-start.6 = (bf16[4,128,128]{2,1,0:T(8,128)(2,1)S(1)}, bf16[4,128,128]{2,1,0:T(8,128)(2,1)}, u32[]{:S(2)}) copy-start(bf16[4,128,128]{2,1,0:T(8,128)(2,1)} %param.11) | copy-start | bytes 393220
  7.2 19.0 %copy-start.3 = (bf16[256,512]{1,0:T(8,128)(2,1)S(1)}, bf16[256,512]{1,0:T(8,128)(2,1)}, u32[]{:S(2)}) copy-start(bf16[256,512]{1,0:T(8,128)(2,1)} %param.7) | copy-start | bytes 786436
  9.4 25.9 %all-to-all-start.1 = ((bf16[32,4,4,256]{3,1,2,0:T(4,128)(2,1)}), bf16[32,4,4,256]{3,1,2,0:T(4,128)(2,1)S(1)}, u32[]{:S(2)}, u32[]{:S(2)}) async-start(bf16[32,4,4,256]{3,1,2,0:T(4,128)(2,1)} %copy.30), calls=%async_computation.1 | async-start | bytes 524288 | tf_op jit(solution)/shard_map/all_to_all | solution.py:64
  35.4 16.2 %all-to-all-start = ((bf16[32,4,4,256]{3,1,2,0:T(4,128)(2,1)}), bf16[32,4,4,256]{3,1,2,0:T(4,128)(2,1)S(1)}, u32[]{:S(2)}, u32[]{:S(2)}) async-start(bf16[32,4,4,256]{3,1,2,0:T(4,128)(2,1)} %bitcast.96), calls=%async_computation | async-start | bytes 524288 | tf_op jit(solution)/shard_map/all_to_all | solution.py:74
  51.6 2.3 copy-start.5
  56.7 16.2 %all-to-all-start.2 = ((bf16[32,4,4,256]{3,1,2,0:T(4,128)(2,1)}), bf16[32,4,4,256]{3,1,2,0:T(4,128)(2,1)S(1)}, u32[]{:S(2)}, u32[]{:S(2)}) async-start(bf16[32,4,4,256]{3,1,2,0:T(4,128)(2,1)} %bitcast.101), calls=%async_computation.2 | async-start | bytes 524288 | tf_op jit(solution)/shard_map/all_to_all | solution.py:77
  73.0 16.9 %all-to-all-start.3 = ((bf16[32,4,4,256]{3,1,2,0:T(4,128)(2,1)}), bf16[32,4,4,256]{3,1,2,0:T(4,128)(2,1)}, u32[]{:S(2)}, u32[]{:S(2)}) async-start(bf16[32,4,4,256]{3,1,2,0:T(4,128)(2,1)} %copy.37), calls=%async_computation.3 | async-start | bytes 524288 | tf_op jit(solution)/shard_map/all_to_all | solution.py:67
  80.7 339.1 %all-reduce.7.cloned.1.call-start = ((), (), s32[]{:S(2)}) async-start(), calls=%async_computation.4 | async-start | bytes 2424832
  82.4 2.2 copy-start.2
  82.4 7.6 %copy-start.4 = (bf16[256,512]{1,0:T(8,128)(2,1)S(1)}, bf16[256,512]{1,0:T(8,128)(2,1)}, u32[]{:S(2)}) copy-start(bf16[256,512]{1,0:T(8,128)(2,1)} %param.7) | copy-start | bytes 786436
  84.6 9.9 %copy-start.1 = (bf16[4,128,128]{2,1,0:T(8,128)(2,1)S(1)}, bf16[4,128,128]{2,1,0:T(8,128)(2,1)}, u32[]{:S(2)}) copy-start(bf16[4,128,128]{2,1,0:T(8,128)(2,1)} %param.8) | copy-start | bytes 393220
Sparse Core Ops, SparseCore 0:
  92.0 327.7 all-reduce.6
where the time goes:
time: 432 us; the launch traced here: 431 us
  waiting for transfers between devices  349 us (81%)
  starting transfers between devices  38.5 us (9%)
  between operations  15.5 us (4%)
  local copies, waits for them, and re-layouts  12.9 us (3%)
  matrix products  12.1 us (3%)
    unnamed x2, waiting for transfers between devices  324 us
    all_to_all x1, starting transfers between devices, body(): lax.all_to_all(send_first, 'blk', split_axis=0, concat_axis=2, tiled=True)  16.7 us
    all_to_all x1, waiting for transfers between devices, body(): lax.all_to_all(send_mixed, 'blk', split_axis=0, concat_axis=2, tiled=True)  8.82 us
  transfers between devices with their start and end apart: 5, of which 5 were waited for; matrix products, arithmetic and copies ran while one was open for 3% of the time, Pallas kernels for 0%

commit v1 on v0

v1 whole, which is shorter than its diff:
```python
import functools

import jax
import jax.numpy as jnp
from jax import lax
from jax.experimental import pallas as pl
from jax.experimental.pallas import tpu as pltpu
from jax.sharding import PartitionSpec as P

MESH = pl.DeviceIdType.MESH
F32 = jnp.float32
BF16 = jnp.bfloat16
PAD = 16


def dot(left, right, left_dim=1, right_dim=0):
    return lax.dot_general(
        left, right, (((left_dim,), (right_dim,)), ((), ())), preferred_element_type=F32
    )


def one_hot(shape, target):
    rows = lax.broadcasted_iota(jnp.int32, (shape[0], 1), 0)
    cols = lax.broadcasted_iota(jnp.int32, shape, 1)
    return jnp.where(cols == target(rows), 1.0, 0.0).astype(BF16)


def pick_rows(wide, groups, width):
    group = (lax.broadcasted_iota(jnp.int32, (wide.shape[0], 1), 0) >> 2) & 3
    picked = wide[:, :width]
    for index in range(1, groups):
        picked = jnp.where(group == index, wide[:, index * width : (index + 1) * width], picked)
    return picked


def send_all(axis, count, me, src, dst, send_sem, recv_sem):
    def step(offset, carry):
        target = lax.rem(me + offset, count)
        pltpu.make_async_remote_copy(
            src_ref=src.at[target],
            dst_ref=dst.at[me],
            send_sem=send_sem,
            recv_sem=recv_sem,
            device_id={axis: target},
            device_id_type=MESH,
        ).start()
        return carry

    lax.fori_loop(1, count, step, 0)
    dst[me] = src[me]


def wait_all(count, ref, sem):
    block = ref.at[pl.ds(0, count - 1)]
    pltpu.make_async_copy(block, block, sem).wait()


def kernel(
    blk_count,
    dp_count,
    factor,
    tok,
    cot,
    up_one,
    up_two,
    down_one,
    down_two,
    grad_tok,
    grad_up_one,
    grad_up_two,
    grad_down_one,
    grad_down_two,
    fwd_out,
    fwd_in,
    bwd_out,
    bwd_in,
    send,
    recv,
    early_send,
    early_recv,
    late_send,
    late_recv,
    wide,
    stack,
    perm,
    grad_down,
    tok_flip,
    pre_act,
    activated,
    slope,
    grad_pre,
    grad_two,
    up_wide,
    up_flip,
    down_wide,
    down_flip,
    spread,
    send_sems,
    recv_sems,
):
    groups, size, hidden = up_two.shape
    total = groups * size
    tokens = tok.shape[0]
    bits = size.bit_length() - 1
    unit = hidden // dp_count
    hidden_pad = dp_count * PAD
    me_blk = lax.axis_index("blk")
    me_dp = lax.axis_index("dp")

    barrier = pltpu.get_barrier_semaphore()
    for axis, count, me in (("blk", blk_count, me_blk), ("dp", dp_count, me_dp)):

        def greet(offset, carry, axis=axis, count=count, me=me):
            pl.semaphore_signal(
                barrier,
                inc=1,
                device_id={axis: lax.rem(me + offset, count)},
                device_id_type=MESH,
            )
            return carry

        lax.fori_loop(1, count, greet, 0)

    square = (total, total)
    fwd_out[...] = one_hot(square, lambda r: ((r & 3) << bits) + ((r >> 4) << 2) + ((r >> 2) & 3))
    for b in range(groups):
        cols = pl.ds(b * size, size)
        wide[:, cols] = dot(tok[:, cols], up_one[b]).astype(BF16)
    send[0] = dot(fwd_out[...], wide[...], 1, 1).astype(BF16).reshape(send.shape[1:])
    pl.semaphore_wait(barrier, blk_count + dp_count - 2)
    send_all("blk", blk_count, me_blk, send.at[0], recv.at[0], send_sems.at[0], recv_sems.at[0])

    bwd_out[...] = one_hot(square, lambda r: (((r >> 2) & 3) << bits) + ((r >> 4) << 2) + (r & 3))
    for c in range(groups):
        cols = pl.ds(c * size, size)
        wide[:, cols] = dot(cot[:, cols], down_two[c], 1, 1).astype(BF16)
    send[1] = dot(bwd_out[...], wide[...], 1, 1).astype(BF16).reshape(send.shape[1:])
    send_all("blk", blk_count, me_blk, send.at[1], recv.at[1], send_sems.at[1], recv_sems.at[1])

    low = size - 1
    fwd_in[...] = one_hot(
        square, lambda r: (((r & low) >> 2) << 4) + ((r >> bits) << 2) + (r & 3)
    )
    bwd_in[...] = one_hot(
        square, lambda r: (((r & low) >> 2) << 4) + ((r & 3) << 2) + (r >> bits)
    )
    spread[...] = one_hot(
        (hidden_pad, hidden),
        lambda r: jnp.where((r & (PAD - 1)) < unit, (r >> 4) * unit + (r & (PAD - 1)), -1),
    )
    eye = one_hot((size, size), lambda r: r)
    for c in range(groups):
        up_wide[c] = dot(up_two[c], spread[...], 1, 1).astype(BF16)
        up_flip[c] = dot(spread[...], up_two[c], 1, 1).astype(BF16)
        down_wide[c] = dot(spread[...], down_one[c]).astype(BF16)
        down_flip[c] = dot(eye, down_wide[c], 1, 1).astype(BF16)
    tok_flip[...] = dot(bwd_out[...], tok[...], 1, 1).astype(BF16)

    wait_all(blk_count, recv.at[0], recv_sems.at[0])
    perm[...] = dot(fwd_in[...], recv[0].reshape(total, tokens)).astype(BF16)
    rows_step = 32
    for c in range(groups):
        rows = pl.ds(c * size, size)
        pre_act[...] = dot(up_flip[c], perm[rows, :])

        def gelu(step, carry, c=c):
            part = pl.ds(pl.multiple_of(step * rows_step, rows_step), rows_step)
            value = pre_act[part, :]
            square_value = value * value
            tangent = jnp.tanh(0.7978845608 * (value + 0.044715 * square_value * value))
            half = 0.5 * (1.0 + tangent)
            activated[c, part, :] = (value * half).astype(BF16)
            slope[c, part, :] = half + 0.5 * value * (1.0 - tangent * tangent) * 0.7978845608 * (
                1.0 + 3.0 * 0.044715 * square_value
            )
            return carry

        lax.fori_loop(0, hidden_pad // rows_step, gelu, 0)
        stack[rows, :] = dot(down_flip[c], activated[c]).astype(BF16)
    send[2] = dot(fwd_out[...], stack[...]).astype(BF16).reshape(send.shape[1:])
    send_all("blk", blk_count, me_blk, send.at[2], recv.at[2], send_sems.at[2], recv_sems.at[2])

    wait_all(blk_count, recv.at[1], recv_sems.at[1])
    grad_down[...] = dot(bwd_in[...], recv[1].reshape(total, tokens)).astype(BF16)
    for c in range(groups):
        rows = pl.ds(c * size, size)
        grad_pre[c] = (dot(down_wide[c], grad_down[rows, :]) * slope[c]).astype(BF16)
        stack[rows, :] = dot(up_wide[c], grad_pre[c]).astype(BF16)
    send[3] = dot(bwd_out[...], stack[...]).astype(BF16).reshape(send.shape[1:])
    send_all("blk", blk_count, me_blk, send.at[3], recv.at[3], send_sems.at[3], recv_sems.at[3])

    for c in range(groups):
        rows = pl.ds(c * size, size)
        term = dot(activated[c], grad_down[rows, :], 1, 1).astype(BF16)
        early_send[:, pl.ds(c * PAD, PAD), :] = term.reshape(dp_count, PAD, size)
        grad_two[rows, :] = dot(perm[rows, :], grad_pre[c], 1, 1).astype(BF16)
    mixed_rows = dot(bwd_out[...], grad_two[...]).astype(BF16)
    for tile in range(hidden_pad // size):
        early_send[:, pl.ds((groups + tile) * PAD, PAD), :] = mixed_rows[
            :, tile * size : (tile + 1) * size
        ].reshape(dp_count, PAD, size)
    send_all("dp", dp_count, me_dp, early_send, early_recv, send_sems.at[4], recv_sems.at[4])

    wait_all(blk_count, recv.at[2], recv_sems.at[2])
    every = dot(recv[2].reshape(total, tokens), cot[...])
    late_send[0] = pick_rows(every, groups, size).astype(BF16).reshape(late_send.shape[1:])
    send_all(
        "dp", dp_count, me_dp, late_send.at[0], late_recv.at[0], send_sems.at[5], recv_sems.at[5]
    )

    wait_all(blk_count, recv.at[3], recv_sems.at[3])
    wide[...] = dot(recv[3].reshape(total, tokens), fwd_out[...], 0, 0).astype(BF16)
    every = dot(tok_flip[...], wide[...])
    late_send[1] = pick_rows(every, groups, size).astype(BF16).reshape(late_send.shape[1:])
    send_all(
        "dp", dp_count, me_dp, late_send.at[1], late_recv.at[1], send_sems.at[6], recv_sems.at[6]
    )
    for b in range(groups):
        cols = pl.ds(b * size, size)
        grad_tok[:, cols] = dot(wide[:, cols], up_one[b], 1, 1).astype(BF16)

    wait_all(dp_count, early_recv, recv_sems.at[4])
    for c in range(groups):
        term = jnp.sum(early_recv[:, pl.ds(c * PAD, PAD), :].astype(F32), axis=0) * factor
        grad_down_one[c] = term[:unit]
    tiles = []
    for tile in range(hidden_pad // size):
        part = early_recv[:, pl.ds((groups + tile) * PAD, PAD), :]
        tiles.append(jnp.sum(part.astype(F32), axis=0) * factor)
    summed = jnp.concatenate(tiles, axis=1)
    summed = lax.dot_general(
        summed,
        spread[...].astype(F32),
        (((1,), (0,)), ((), ())),
        precision=lax.Precision.HIGHEST,
        preferred_element_type=F32,
    )
    unit_rows = size // dp_count
    for c in range(groups):
        grad_up_two[c] = summed[c * unit_rows : (c + 1) * unit_rows]
    wait_all(dp_count, late_recv.at[0], recv_sems.at[5])
    term = jnp.sum(late_recv[0].astype(F32), axis=0) * factor
    for c in range(groups):
        grad_down_two[c] = term[c * unit_rows : (c + 1) * unit_rows]
    wait_all(dp_count, late_recv.at[1], recv_sems.at[6])
    term = jnp.sum(late_recv[1].astype(F32), axis=0) * factor
    for c in range(groups):
        grad_up_one[c] = term[c * unit_rows : (c + 1) * unit_rows]

    for index in range(4):
        wait_all(blk_count, send.at[index], send_sems.at[index])
    wait_all(dp_count, early_send, send_sems.at[4])
    for index in range(2):
        wait_all(dp_count, late_send.at[index], send_sems.at[5 + index])


def body(tok, cot, up_one, up_two, down_one, down_two):
    groups, size, hidden = up_two.shape
    tokens = tok.shape[0]
    blk_count = lax.axis_size("blk")
    dp_count = lax.axis_size("dp")
    total = groups * size
    hidden_pad = dp_count * PAD
    unit_rows = size // dp_count
    factor = float(tokens * dp_count) ** (-0.5)
    chunk = groups * groups
    vmem = pl.BlockSpec(memory_space=pltpu.VMEM)
    shapes = [
        ((total, total), BF16),
        ((total, total), BF16),
        ((total, total), BF16),
        ((total, total), BF16),
        ((4, blk_count, chunk, tokens), BF16),
        ((4, blk_count, chunk, tokens), BF16),
        ((dp_count, (groups + hidden_pad // size) * PAD, size), BF16),
        ((dp_count, (groups + hidden_pad // size) * PAD, size), BF16),
        ((2, dp_count, chunk, size), BF16),
        ((2, dp_count, chunk, size), BF16),
        ((tokens, total), BF16),
        ((total, tokens), BF16),
        ((total, tokens), BF16),
        ((total, tokens), BF16),
        ((total, tokens), BF16),
        ((hidden_pad, tokens), F32),
        ((groups, hidden_pad, tokens), BF16),
        ((groups, hidden_pad, tokens), F32),
        ((groups, hidden_pad, tokens), BF16),
        ((total, hidden_pad), BF16),
        ((groups, size, hidden_pad), BF16),
        ((groups, hidden_pad, size), BF16),
        ((groups, hidden_pad, size), BF16),
        ((groups, size, hidden_pad), BF16),
        ((hidden_pad, hidden), BF16),
    ]
    return pl.pallas_call(
        functools.partial(kernel, blk_count, dp_count, factor),
        out_shape=(
            jax.ShapeDtypeStruct((tokens, total), BF16),
            jax.ShapeDtypeStruct((groups, unit_rows, size), F32),
            jax.ShapeDtypeStruct((groups, unit_rows, hidden), F32),
            jax.ShapeDtypeStruct((groups, hidden // dp_count, size), F32),
            jax.ShapeDtypeStruct((groups, unit_rows, size), F32),
        ),
        in_specs=[vmem] * 6,
        out_specs=(vmem,) * 5,
        scratch_shapes=[pltpu.VMEM(shape, kind) for shape, kind in shapes]
        + [pltpu.SemaphoreType.DMA((7,)), pltpu.SemaphoreType.DMA((7,))],
        compiler_params=pltpu.CompilerParams(
            collective_id=0, has_side_effects=True, vmem_limit_bytes=48 * 1024 * 1024
        ),
    )(tok, cot, up_one, up_two, down_one, down_two)


def solution(mesh):
    in_specs = (P("dp", "blk"), P("dp", "blk")) + (P("blk", None, None),) * 4
    out_specs = (P("dp", "blk"),) + (P("blk", "dp", None),) * 4
    return jax.shard_map(body, mesh=mesh, in_specs=in_specs, out_specs=out_specs, check_vma=False)
```

time: 432 us -> 101 us (0.23)
  the two profiles are of different devices: /device:TPU:12 before, /device:TPU:1 now
where the time goes in v1:
time: 101 us
  Pallas kernels  94.1 us (93%)
  local copies, waits for them, and re-layouts  6.24 us (6%)
    pallas_call x1, Pallas kernels, body(): pl.pallas_call(functools.partial(kernel, blk_count, dp_count, factor), ou...  94.1 us
    unnamed x15, local copies, waits for them, and re-layouts  5.62 us

profile of v1, /device:TPU:1, one launch (start us, length us, event | category | flops | bytes accessed | tf_op | source)
XLA Modules:
  0.0 101.1 jit_solution(3759273288352355735)
XLA Ops:
  0.6 0.0 copy-start
  0.6 0.0 copy-start.2
  0.7 0.0 copy-start.1
  0.7 1.3 %copy.11.up_two = bf16[4,128,416]{2,1,0:T(8,128)(2,1)S(1)} copy(bf16[4,128,416]{1,2,0:T(8,128)(2,1)} %param.9) | data formatting | bytes 851968 | tf_op args[3]
  2.0 0.0 copy-done
  2.0 0.0 copy-done.2
  2.0 0.0 copy-done.1
  2.0 0.0 copy-start.3
  2.0 0.9 copy-done.3
  2.9 0.0 copy-start.4
  2.9 0.9 copy-done.4
  3.8 94.1 %shard_map.101 = (bf16[256,512]{1,0:T(8,128)(2,1)S(1)}, f32[4,4,128]{2,1,0:T(4,128)S(1)}, f32[4,4,416]{2,1,0:T(4,128)S(1)}, f32[4,13,128]{2,1,0:T(8,128)S(1)}, f32[4,4,128]{2,1,0:T(4,128)S(1)}) custom-call(bf16[256,512]{1,0:T(8,128)(2,1)S(1)} %copy-done.1, bf16[256,512]{1,0:T(8,128)(2,1)S(1)} %copy-done.2, bf16[4,128,128]{2,1,0:T(8,128)(2,1)S(1)} %copy-done.3, ...), custom_call_target="tpu_custom_call" | custom-call | tf_op jit(solution)/shard_map/pallas_call | solution.py:295
  97.9 0.6 copy.12
  98.5 0.7 copy.17
  99.2 0.6 copy.18
  99.8 0.6 copy.19
  100.5 0.6 copy.20
Async XLA Ops:
  0.6 1.3 %copy-start = (bf16[4,416,128]{2,1,0:T(8,128)(2,1)S(1)}, bf16[4,416,128]{2,1,0:T(8,128)(2,1)}, u32[]{:S(2)}) copy-start(bf16[4,416,128]{2,1,0:T(8,128)(2,1)} %down_one.1) | copy-start | bytes 1277956
  0.6 1.3 %copy-start.2 = (bf16[256,512]{1,0:T(8,128)(2,1)S(1)}, bf16[256,512]{1,0:T(8,128)(2,1)}, u32[]{:S(2)}) copy-start(bf16[256,512]{1,0:T(8,128)(2,1)} %cot.1) | copy-start | bytes 786436
  0.7 1.3 %copy-start.1 = (bf16[256,512]{1,0:T(8,128)(2,1)S(1)}, bf16[256,512]{1,0:T(8,128)(2,1)}, u32[]{:S(2)}) copy-start(bf16[256,512]{1,0:T(8,128)(2,1)} %tok.1) | copy-start | bytes 786436
  2.0 0.9 copy-start.3
  2.9 0.9 copy-start.4

commit v2 on v1

v2 whole, which is shorter than its diff:
```python
import functools

import jax
import jax.numpy as jnp
from jax import lax
from jax.experimental import pallas as pl
from jax.experimental.pallas import tpu as pltpu
from jax.sharding import PartitionSpec as P

MESH = pl.DeviceIdType.MESH
F32 = jnp.float32
BF16 = jnp.bfloat16
PAD = 16


def dot(left, right, left_dim=1, right_dim=0):
    return lax.dot_general(
        left, right, (((left_dim,), (right_dim,)), ((), ())), preferred_element_type=F32
    )


def one_hot(shape, target):
    rows = lax.broadcasted_iota(jnp.int32, (shape[0], 1), 0)
    cols = lax.broadcasted_iota(jnp.int32, shape, 1)
    return jnp.where(cols == target(rows), 1.0, 0.0).astype(BF16)


def pick_rows(wide, groups, width):
    group = (lax.broadcasted_iota(jnp.int32, (wide.shape[0], 1), 0) >> 2) & 3
    picked = wide[:, :width]
    for index in range(1, groups):
        picked = jnp.where(group == index, wide[:, index * width : (index + 1) * width], picked)
    return picked


def send_all(axis, me, count, peer, src, dst, send_sem, recv_sem):
    def step(offset, carry):
        target = lax.rem(me + offset, count)
        pltpu.make_async_remote_copy(
            src_ref=src(target),
            dst_ref=dst.at[me],
            send_sem=send_sem,
            recv_sem=recv_sem,
            device_id={axis: peer(target)},
            device_id_type=MESH,
        ).start()
        return carry

    lax.fori_loop(1, count, step, 0)
    dst[me] = src(me)[...]


def wait_all(block, sem):
    pltpu.make_async_copy(block, block, sem).wait()


def add_up(ref):
    return jnp.sum(ref[...].astype(F32), axis=0)


def kernel(
    blk_count,
    dp_count,
    factor,
    tok_hbm,
    cot_hbm,
    up_one_hbm,
    up_two_hbm,
    down_one_hbm,
    down_two_hbm,
    grad_tok,
    grad_up_one,
    grad_up_two,
    grad_down_one,
    grad_down_two,
    tok,
    cot,
    up_one,
    up_two,
    down_one,
    down_two,
    fwd_out,
    fwd_in,
    bwd_out,
    bwd_in,
    send,
    recv,
    dn_send,
    dn_recv,
    dn_mid,
    dn_last,
    up_send,
    up_recv,
    up_mid,
    up_last,
    late_send,
    late_recv,
    late_mid,
    late_last,
    wide,
    stack,
    perm,
    grad_down,
    tok_flip,
    pre_act,
    activated,
    slope,
    grad_pre,
    grad_two,
    up_wide,
    up_flip,
    down_wide,
    down_flip,
    spread,
    send_sems,
    recv_sems,
    load_sems,
):
    groups, hidden, size = up_two.shape
    total = groups * size
    tokens = tok.shape[0]
    bits = size.bit_length() - 1
    unit = hidden // dp_count
    hidden_pad = dp_count * PAD
    me_blk = lax.axis_index("blk")
    me_dp = lax.axis_index("dp")

    across = dn_send.shape[1]
    along = dn_send.shape[0]
    me_y = lax.rem(me_dp, across)
    me_z = me_dp // across

    def same(index):
        return index

    def z_peer(index):
        return index * across + me_y

    def y_peer(index):
        return me_z * across + index

    pairs = (
        (tok_hbm, tok),
        (up_one_hbm, up_one),
        (cot_hbm, cot),
        (down_two_hbm, down_two),
        (up_two_hbm, up_two),
        (down_one_hbm, down_one),
    )
    loads = [
        pltpu.make_async_copy(src, dst, load_sems.at[index])
        for index, (src, dst) in enumerate(pairs)
    ]
    loads[0].start()
    loads[1].start()
    barrier = pltpu.get_barrier_semaphore()
    rings = (
        ("blk", me_blk, blk_count, same),
        ("dp", me_z, along, z_peer),
        ("dp", me_y, across, y_peer),
    )
    for axis, me, count, peer in rings:

        def greet(offset, carry, axis=axis, me=me, count=count, peer=peer):
            pl.semaphore_signal(
                barrier,
                inc=1,
                device_id={axis: peer(lax.rem(me + offset, count))},
                device_id_type=MESH,
            )
            return carry

        lax.fori_loop(1, count, greet, 0)
    for load in loads[2:]:
        load.start()

    def exchange(index):
        send_all(
            "blk",
            me_blk,
            blk_count,
            same,
            lambda target: send.at[index, target],
            recv.at[index],
            send_sems.at[index],
            recv_sems.at[index],
        )

    def arrive(index):
        wait_all(recv.at[index, pl.ds(0, blk_count - 1)], recv_sems.at[index])
        return recv[index].reshape(total, tokens)

    square = (total, total)
    fwd_out[...] = one_hot(square, lambda r: ((r & 3) << bits) + ((r >> 4) << 2) + ((r >> 2) & 3))
    loads[0].wait()
    loads[1].wait()
    for b in range(groups):
        cols = pl.ds(b * size, size)
        wide[:, cols] = dot(tok[:, cols], up_one[b]).astype(BF16)
    send[0] = dot(fwd_out[...], wide[...], 1, 1).astype(BF16).reshape(send.shape[1:])
    pl.semaphore_wait(barrier, blk_count + along + across - 3)
    exchange(0)

    bwd_out[...] = one_hot(square, lambda r: (((r >> 2) & 3) << bits) + ((r >> 4) << 2) + (r & 3))
    loads[2].wait()
    loads[3].wait()
    for c in range(groups):
        cols = pl.ds(c * size, size)
        wide[:, cols] = dot(cot[:, cols], down_two[c], 1, 1).astype(BF16)
    send[1] = dot(bwd_out[...], wide[...], 1, 1).astype(BF16).reshape(send.shape[1:])
    exchange(1)

    low = size - 1
    fwd_in[...] = one_hot(
        square, lambda r: (((r & low) >> 2) << 4) + ((r >> bits) << 2) + (r & 3)
    )
    bwd_in[...] = one_hot(
        square, lambda r: (((r & low) >> 2) << 4) + ((r & 3) << 2) + (r >> bits)
    )
    spread[...] = one_hot(
        (hidden_pad, hidden),
        lambda r: jnp.where((r & (PAD - 1)) < unit, (r >> 4) * unit + (r & (PAD - 1)), -1),
    )
    eye = one_hot((size, size), lambda r: r)
    loads[4].wait()
    loads[5].wait()
    for c in range(groups):
        up_flip[c] = dot(spread[...], up_two[c]).astype(BF16)
        up_wide[c] = dot(eye, up_flip[c], 1, 1).astype(BF16)
        down_wide[c] = dot(spread[...], down_one[c]).astype(BF16)
        down_flip[c] = dot(eye, down_wide[c], 1, 1).astype(BF16)
    tok_flip[...] = dot(bwd_out[...], tok[...], 1, 1).astype(BF16)

    perm[...] = dot(fwd_in[...], arrive(0)).astype(BF16)
    rows_step = 32
    for c in range(groups):
        rows = pl.ds(c * size, size)
        pre_act[...] = dot(up_flip[c], perm[rows, :])

        def gelu(step, carry, c=c):
            part = pl.ds(pl.multiple_of(step * rows_step, rows_step), rows_step)
            value = pre_act[part, :]
            square_value = value * value
            tangent = jnp.tanh(0.7978845608 * (value + 0.044715 * square_value * value))
            half = 0.5 * (1.0 + tangent)
            activated[c, part, :] = (value * half).astype(BF16)
            slope[c, part, :] = half + 0.5 * value * (1.0 - tangent * tangent) * 0.7978845608 * (
                1.0 + 3.0 * 0.044715 * square_value
            )
            return carry

        lax.fori_loop(0, hidden_pad // rows_step, gelu, 0)
        stack[rows, :] = dot(down_flip[c], activated[c]).astype(BF16)
    send[2] = dot(fwd_out[...], stack[...]).astype(BF16).reshape(send.shape[1:])
    exchange(2)

    grad_down[...] = dot(bwd_in[...], arrive(1)).astype(BF16)
    for c in range(groups):
        rows = pl.ds(c * size, size)
        grad_pre[c] = (dot(down_wide[c], grad_down[rows, :]) * slope[c]).astype(BF16)
        stack[rows, :] = dot(up_wide[c], grad_pre[c]).astype(BF16)
    send[3] = dot(bwd_out[...], stack[...]).astype(BF16).reshape(send.shape[1:])
    exchange(3)

    for c in range(groups):
        rows = pl.ds(c * size, size)
        term = dot(activated[c], grad_down[rows, :], 1, 1).astype(BF16)
        dn_send[:, :, pl.ds(c * PAD, PAD), :] = term.reshape(along, across, PAD, size)
    send_all(
        "dp",
        me_z,
        along,
        z_peer,
        lambda target: dn_send.at[target],
        dn_recv,
        send_sems.at[4],
        recv_sems.at[4],
    )
    for c in range(groups):
        rows = pl.ds(c * size, size)
        grad_two[rows, :] = dot(perm[rows, :], grad_pre[c], 1, 1).astype(BF16)
    mixed_rows = dot(bwd_out[...], grad_two[...]).astype(BF16)
    tiles = hidden_pad // size
    for tile in range(tiles):
        up_send[:, :, pl.ds(tile * PAD, PAD), :] = mixed_rows[
            :, tile * size : (tile + 1) * size
        ].reshape(along, across, PAD, size)
    send_all(
        "dp",
        me_y,
        across,
        y_peer,
        lambda target: up_send.at[:, target],
        up_recv,
        send_sems.at[5],
        recv_sems.at[5],
    )

    def late(index, every):
        late_send[index] = (
            pick_rows(every, groups, size).astype(BF16).reshape(late_send.shape[1:])
        )
        send_all(
            "dp",
            me_z,
            along,
            z_peer,
            lambda target: late_send.at[index, target],
            late_recv.at[index],
            send_sems.at[6 + index],
            recv_sems.at[6 + index],
        )

    late(0, dot(arrive(2), cot[...]))
    wide[...] = dot(arrive(3), fwd_out[...], 0, 0).astype(BF16)
    late(1, dot(tok_flip[...], wide[...]))
    for b in range(groups):
        cols = pl.ds(b * size, size)
        grad_tok[:, cols] = dot(wide[:, cols], up_one[b], 1, 1).astype(BF16)

    wait_all(dn_recv.at[pl.ds(0, along - 1)], recv_sems.at[4])
    dn_mid[...] = add_up(dn_recv).astype(BF16)
    send_all(
        "dp",
        me_y,
        across,
        y_peer,
        lambda target: dn_mid.at[target],
        dn_last,
        send_sems.at[8],
        recv_sems.at[8],
    )
    wait_all(up_recv.at[pl.ds(0, across - 1)], recv_sems.at[5])
    up_mid[...] = add_up(up_recv).astype(BF16)
    send_all(
        "dp",
        me_z,
        along,
        z_peer,
        lambda target: up_mid.at[target],
        up_last,
        send_sems.at[9],
        recv_sems.at[9],
    )
    for index in range(2):
        wait_all(late_recv.at[index, pl.ds(0, along - 1)], recv_sems.at[6 + index])
        late_mid[:, pl.ds(index * PAD, PAD), :] = add_up(late_recv.at[index]).astype(BF16)
    send_all(
        "dp",
        me_y,
        across,
        y_peer,
        lambda target: late_mid.at[target],
        late_last,
        send_sems.at[10],
        recv_sems.at[10],
    )

    unit_rows = size // dp_count
    wait_all(dn_last.at[pl.ds(0, across - 1)], recv_sems.at[8])
    summed = add_up(dn_last) * factor
    for c in range(groups):
        grad_down_one[:, c, :] = summed[c * PAD : c * PAD + unit]
    wait_all(up_last.at[pl.ds(0, along - 1)], recv_sems.at[9])
    summed = add_up(up_last) * factor
    summed = lax.dot_general(
        jnp.concatenate([summed[tile * PAD : (tile + 1) * PAD] for tile in range(tiles)], axis=1),
        spread[...].astype(F32),
        (((1,), (0,)), ((), ())),
        precision=lax.Precision.HIGHEST,
        preferred_element_type=F32,
    )
    for c in range(groups):
        grad_up_two[c] = summed[c * unit_rows : (c + 1) * unit_rows]
    wait_all(late_last.at[pl.ds(0, across - 1)], recv_sems.at[10])
    summed = add_up(late_last) * factor
    for c in range(groups):
        grad_down_two[c] = summed[c * unit_rows : (c + 1) * unit_rows]
        grad_up_one[c] = summed[PAD + c * unit_rows : PAD + (c + 1) * unit_rows]

    for index in range(4):
        wait_all(send.at[index, pl.ds(0, blk_count - 1)], send_sems.at[index])
    wait_all(dn_send.at[pl.ds(0, along - 1)], send_sems.at[4])
    wait_all(up_send.at[:, pl.ds(0, across - 1)], send_sems.at[5])
    for index in range(2):
        wait_all(late_send.at[index, pl.ds(0, along - 1)], send_sems.at[6 + index])
    wait_all(dn_mid.at[pl.ds(0, across - 1)], send_sems.at[8])
    wait_all(up_mid.at[pl.ds(0, along - 1)], send_sems.at[9])
    wait_all(late_mid.at[pl.ds(0, across - 1)], send_sems.at[10])


def store(*refs):
    count = len(refs) // 2
    copies = [
        pltpu.make_async_copy(refs[index], refs[count + index], refs[-1].at[index])
        for index in range(count)
    ]
    for copy in copies:
        copy.start()
    for copy in copies:
        copy.wait()


def body(tok, cot, up_one, up_two, down_one, down_two):
    groups, size, hidden = up_two.shape
    up_two = jnp.swapaxes(up_two, 1, 2)
    tokens = tok.shape[0]
    blk_count = lax.axis_size("blk")
    dp_count = lax.axis_size("dp")
    total = groups * size
    hidden_pad = dp_count * PAD
    unit_rows = size // dp_count
    factor = float(tokens * dp_count) ** (-0.5)
    chunk = groups * groups
    across = 4 if dp_count % 8 == 0 else 2
    along = dp_count // across
    rows = groups * PAD
    vmem = pl.BlockSpec(memory_space=pltpu.VMEM)
    hbm = pl.BlockSpec(memory_space=pl.ANY)
    shapes = [(arg.shape, BF16) for arg in (tok, cot, up_one, up_two, down_one, down_two)]
    shapes += [
        ((total, total), BF16),
        ((total, total), BF16),
        ((total, total), BF16),
        ((total, total), BF16),
        ((4, blk_count, chunk, tokens), BF16),
        ((4, blk_count, chunk, tokens), BF16),
        ((along, across, rows, size), BF16),
        ((along, across, rows, size), BF16),
        ((across, rows, size), BF16),
        ((across, rows, size), BF16),
        ((along, across, rows, size), BF16),
        ((across, along, rows, size), BF16),
        ((along, rows, size), BF16),
        ((along, rows, size), BF16),
        ((2, along, across, chunk, size), BF16),
        ((2, along, across, chunk, size), BF16),
        ((across, 2 * chunk, size), BF16),
        ((across, 2 * chunk, size), BF16),
        ((tokens, total), BF16),
        ((total, tokens), BF16),
        ((total, tokens), BF16),
        ((total, tokens), BF16),
        ((total, tokens), BF16),
        ((hidden_pad, tokens), F32),
        ((groups, hidden_pad, tokens), BF16),
        ((groups, hidden_pad, tokens), F32),
        ((groups, hidden_pad, tokens), BF16),
        ((total, hidden_pad), BF16),
        ((groups, size, hidden_pad), BF16),
        ((groups, hidden_pad, size), BF16),
        ((groups, hidden_pad, size), BF16),
        ((groups, size, hidden_pad), BF16),
        ((hidden_pad, hidden), BF16),
    ]
    outs = (
        jax.ShapeDtypeStruct((tokens, total), BF16),
        jax.ShapeDtypeStruct((groups, unit_rows, size), F32),
        jax.ShapeDtypeStruct((groups, unit_rows, hidden), F32),
        jax.ShapeDtypeStruct((hidden // dp_count, groups, size), F32),
        jax.ShapeDtypeStruct((groups, unit_rows, size), F32),
    )
    results = pl.pallas_call(
        functools.partial(kernel, blk_count, dp_count, factor),
        out_shape=outs,
        in_specs=[hbm] * 6,
        out_specs=(vmem,) * 5,
        scratch_shapes=[pltpu.VMEM(shape, kind) for shape, kind in shapes]
        + [
            pltpu.SemaphoreType.DMA((11,)),
            pltpu.SemaphoreType.DMA((11,)),
            pltpu.SemaphoreType.DMA((6,)),
        ],
        compiler_params=pltpu.CompilerParams(
            collective_id=0, has_side_effects=True, vmem_limit_bytes=60 * 1024 * 1024
        ),
    )(tok, cot, up_one, up_two, down_one, down_two)
    results = pl.pallas_call(
        store,
        out_shape=outs,
        in_specs=[hbm] * 5,
        out_specs=(hbm,) * 5,
        scratch_shapes=[pltpu.SemaphoreType.DMA((5,))],
        compiler_params=pltpu.CompilerParams(vmem_limit_bytes=60 * 1024 * 1024),
    )(*results)
    results = list(results)
    results[3] = jnp.swapaxes(results[3], 0, 1)
    return tuple(results)


def solution(mesh):
    in_specs = (P("dp", "blk"), P("dp", "blk")) + (P("blk", None, None),) * 4
    out_specs = (P("dp", "blk"),) + (P("blk", "dp", None),) * 4
    return jax.shard_map(body, mesh=mesh, in_specs=in_specs, out_specs=out_specs, check_vma=False)
```

time: 101 us -> 77.7 us (0.77); the launches traced: 101 us -> 76.7 us
  Pallas kernels: 94.1 us -> 76 us
  local copies, waits for them, and re-layouts: 6.24 us -> 0 us
    pallas_call x1, Pallas kernels: 94.1 us -> 64.6 us  [body(): pl.pallas_call(functools.partial(kernel, blk_count, dp_count, factor), ou...]
    pallas_call x0 -> x1, Pallas kernels: none -> 11.4 us  [body(): pl.pallas_call(store, out_shape=outs, in_specs=[hbm] * 5, out_specs=(hbm,...]
    unnamed x15 -> x0, local copies, waits for them, and re-layouts: 5.62 us -> none
where the time goes in v2:
time: 77.7 us; the launch traced here: 76.7 us
  Pallas kernels  76 us (98%)
    pallas_call x1, Pallas kernels, body(): pl.pallas_call(functools.partial(kernel, blk_count, dp_count, factor), ou...  64.6 us
    pallas_call x1, Pallas kernels, body(): pl.pallas_call(store, out_shape=outs, in_specs=[hbm] * 5, out_specs=(hbm,...  11.4 us

profile of v2, /device:TPU:1, one launch (start us, length us, event | category | flops | bytes accessed | tf_op | source)
XLA Modules:
  0.0 76.7 jit_solution(17520480874300647043)
XLA Ops:
  0.6 64.6 %shard_map.101 = (bf16[256,512]{1,0:T(8,128)(2,1)}, f32[4,4,128]{2,1,0:T(4,128)}, f32[4,4,416]{2,1,0:T(4,128)}, f32[13,4,128]{2,1,0:T(4,128)}, f32[4,4,128]{2,1,0:T(4,128)}) custom-call(bf16[256,512]{1,0:T(8,128)(2,1)} %tok_hbm.1, bf16[256,512]{1,0:T(8,128)(2,1)} %cot_hbm.1, bf16[4,128,128]{2,1,0:T(8,128)(2,1)} %up_one_hbm.1, bf16[4,416,128]{2,1,0:T(8,128)(2,1)} %bitcast.2, ...), custom_call_target="tpu_custom_call" | custom-call | tf_op jit(solution)/shard_map/pallas_call | solution.py:463
  65.3 11.4 %shard_map.102 = (bf16[256,512]{1,0:T(8,128)(2,1)}, f32[4,4,128]{2,1,0:T(4,128)}, f32[4,4,416]{2,1,0:T(4,128)}, f32[13,4,128]{2,1,0:T(4,128)}, f32[4,4,128]{2,1,0:T(4,128)}) custom-call(bf16[256,512]{1,0:T(8,128)(2,1)} %get-tuple-element.15.refs_0_, f32[4,4,128]{2,1,0:T(4,128)} %get-tuple-element.16.refs_1_, f32[4,4,416]{2,1,0:T(4,128)} %get-tuple-element.17.refs_2_, ...), custom_call_target="tpu_custom_call" | custom-call | tf_op jit(solution)/shard_map/pallas_call | solution.py:478

commit v3 on v2

--- a/solution.py
+++ b/solution.py
@@ -34,7 +34,7 @@
 
 
 def send_all(axis, me, count, peer, src, dst, send_sem, recv_sem):
-    def step(offset, carry):
+    for offset in range(1, count):
         target = lax.rem(me + offset, count)
         pltpu.make_async_remote_copy(
             src_ref=src(target),
@@ -44,9 +44,6 @@
             device_id={axis: peer(target)},
             device_id_type=MESH,
         ).start()
-        return carry
-
-    lax.fori_loop(1, count, step, 0)
     dst[me] = src(me)[...]
 
 
@@ -296,10 +293,8 @@
         recv_sems.at[5],
     )
 
-    def late(index, every):
-        late_send[index] = (
-            pick_rows(every, groups, size).astype(BF16).reshape(late_send.shape[1:])
-        )
+    def late(index, rows):
+        late_send[index] = rows.astype(BF16).reshape(late_send.shape[1:])
         send_all(
             "dp",
             me_z,
@@ -311,9 +306,14 @@
             recv_sems.at[6 + index],
         )
 
-    late(0, dot(arrive(2), cot[...]))
-    wide[...] = dot(arrive(3), fwd_out[...], 0, 0).astype(BF16)
-    late(1, dot(tok_flip[...], wide[...]))
+    late(0, pick_rows(dot(arrive(2), cot[...]), groups, size))
+    across_row = lax.broadcasted_iota(jnp.int32, square, 0)
+    same_group = ((across_row >> 2) & 3) == (lax.broadcasted_iota(jnp.int32, square, 1) & 3)
+    squeeze = one_hot((total, size), lambda r: r >> 2)
+    got = arrive(3)
+    every = jnp.where(same_group, dot(tok_flip[...], got, 1, 1), 0.0).astype(BF16)
+    late(1, dot(every, squeeze))
+    wide[...] = dot(got, fwd_out[...], 0, 0).astype(BF16)
     for b in range(groups):
         cols = pl.ds(b * size, size)
         grad_tok[:, cols] = dot(wide[:, cols], up_one[b], 1, 1).astype(BF16)
@@ -391,14 +391,8 @@
 
 def store(*refs):
     count = len(refs) // 2
-    copies = [
-        pltpu.make_async_copy(refs[index], refs[count + index], refs[-1].at[index])
-        for index in range(count)
-    ]
-    for copy in copies:
-        copy.start()
-    for copy in copies:
-        copy.wait()
+    for index in range(count):
+        refs[count + index][...] = refs[index][...]
 
 
 def body(tok, cot, up_one, up_two, down_one, down_two):
@@ -478,9 +472,6 @@
     results = pl.pallas_call(
         store,
         out_shape=outs,
-        in_specs=[hbm] * 5,
-        out_specs=(hbm,) * 5,
-        scratch_shapes=[pltpu.SemaphoreType.DMA((5,))],
         compiler_params=pltpu.CompilerParams(vmem_limit_bytes=60 * 1024 * 1024),
     )(*results)
     results = list(results)

time: 77.7 us -> 68 us (0.88)
  Pallas kernels: 76 us -> 66.7 us
    pallas_call x1, Pallas kernels: 11.4 us -> 1.72 us  [body(): pl.pallas_call(store, out_shape=outs, compiler_params=pltpu.CompilerParam...]
where the time goes in v3:
time: 68 us; the launch traced here: 67.3 us
  Pallas kernels  66.7 us (98%)
    pallas_call x1, Pallas kernels, body(): pl.pallas_call(functools.partial(kernel, blk_count, dp_count, factor), ou...  65 us
    pallas_call x1, Pallas kernels, body(): pl.pallas_call(store, out_shape=outs, compiler_params=pltpu.CompilerParam...  1.72 us

profile of v3, /device:TPU:1, one launch (start us, length us, event | category | flops | bytes accessed | tf_op | source)
XLA Modules:
  0.0 67.3 jit_solution(8031820442111067445)
XLA Ops:
  0.6 65.0 %shard_map.101 = (bf16[256,512]{1,0:T(8,128)(2,1)}, f32[4,4,128]{2,1,0:T(4,128)}, f32[4,4,416]{2,1,0:T(4,128)}, f32[13,4,128]{2,1,0:T(4,128)}, f32[4,4,128]{2,1,0:T(4,128)}) custom-call(bf16[256,512]{1,0:T(8,128)(2,1)} %tok_hbm.1, bf16[256,512]{1,0:T(8,128)(2,1)} %cot_hbm.1, bf16[4,128,128]{2,1,0:T(8,128)(2,1)} %up_one_hbm.1, bf16[4,416,128]{2,1,0:T(8,128)(2,1)} %bitcast.2, ...), custom_call_target="tpu_custom_call" | custom-call | tf_op jit(solution)/shard_map/pallas_call | solution.py:457
  65.6 1.7 %shard_map.102 = (bf16[256,512]{1,0:T(8,128)(2,1)}, f32[4,4,128]{2,1,0:T(4,128)}, f32[4,4,416]{2,1,0:T(4,128)}, f32[13,4,128]{2,1,0:T(4,128)}, f32[4,4,128]{2,1,0:T(4,128)}) custom-call(bf16[256,512]{1,0:T(8,128)(2,1)} %get-tuple-element.15.refs_0_, f32[4,4,128]{2,1,0:T(4,128)} %get-tuple-element.16.refs_1_, f32[4,4,416]{2,1,0:T(4,128)} %get-tuple-element.17.refs_2_, ...), custom_call_target="tpu_custom_call" | custom-call | tf_op jit(solution)/shard_map/pallas_call | solution.py:472

commit v4 on v3

--- a/solution.py
+++ b/solution.py
@@ -34,7 +34,7 @@
 
 
 def send_all(axis, me, count, peer, src, dst, send_sem, recv_sem):
-    for offset in range(1, count):
+    for offset in sorted(range(1, count), key=lambda hop: -min(hop, count - hop)):
         target = lax.rem(me + offset, count)
         pltpu.make_async_remote_copy(
             src_ref=src(target),
@@ -109,6 +109,7 @@
     down_wide,
     down_flip,
     spread,
+    tok_out,
     send_sems,
     recv_sems,
     load_sems,
@@ -316,7 +317,9 @@
     wide[...] = dot(got, fwd_out[...], 0, 0).astype(BF16)
     for b in range(groups):
         cols = pl.ds(b * size, size)
-        grad_tok[:, cols] = dot(wide[:, cols], up_one[b], 1, 1).astype(BF16)
+        tok_out[:, cols] = dot(wide[:, cols], up_one[b], 1, 1).astype(BF16)
+    tok_store = pltpu.make_async_copy(tok_out, grad_tok, load_sems.at[6])
+    tok_store.start()
 
     wait_all(dn_recv.at[pl.ds(0, along - 1)], recv_sems.at[4])
     dn_mid[...] = add_up(dn_recv).astype(BF16)
@@ -387,6 +390,7 @@
     wait_all(dn_mid.at[pl.ds(0, across - 1)], send_sems.at[8])
     wait_all(up_mid.at[pl.ds(0, along - 1)], send_sems.at[9])
     wait_all(late_mid.at[pl.ds(0, across - 1)], send_sems.at[10])
+    tok_store.wait()
 
 
 def store(*refs):
@@ -446,6 +450,7 @@
         ((groups, hidden_pad, size), BF16),
         ((groups, size, hidden_pad), BF16),
         ((hidden_pad, hidden), BF16),
+        ((tokens, total), BF16),
     ]
     outs = (
         jax.ShapeDtypeStruct((tokens, total), BF16),
@@ -458,12 +463,12 @@
         functools.partial(kernel, blk_count, dp_count, factor),
         out_shape=outs,
         in_specs=[hbm] * 6,
-        out_specs=(vmem,) * 5,
+        out_specs=(hbm,) + (vmem,) * 4,
         scratch_shapes=[pltpu.VMEM(shape, kind) for shape, kind in shapes]
         + [
             pltpu.SemaphoreType.DMA((11,)),
             pltpu.SemaphoreType.DMA((11,)),
-            pltpu.SemaphoreType.DMA((6,)),
+            pltpu.SemaphoreType.DMA((7,)),
         ],
         compiler_params=pltpu.CompilerParams(
             collective_id=0, has_side_effects=True, vmem_limit_bytes=60 * 1024 * 1024

time: 68 us -> 67.2 us (0.988)
  no operation moved by 1% of the time
where the time goes in v4:
time: 67.2 us; the launch traced here: 67 us
  Pallas kernels  66.4 us (99%)
    pallas_call x1, Pallas kernels, body(): pl.pallas_call(functools.partial(kernel, blk_count, dp_count, factor), ou...  64.7 us
    pallas_call x1, Pallas kernels, body(): pl.pallas_call(store, out_shape=outs, compiler_params=pltpu.CompilerParam...  1.72 us

profile of v4, /device:TPU:1, one launch (start us, length us, event | category | flops | bytes accessed | tf_op | source)
XLA Modules:
  0.0 67.0 jit_solution(863110374354274035)
XLA Ops:
  0.6 64.7 %shard_map.101 = (bf16[256,512]{1,0:T(8,128)(2,1)}, f32[4,4,128]{2,1,0:T(4,128)}, f32[4,4,416]{2,1,0:T(4,128)}, f32[13,4,128]{2,1,0:T(4,128)}, f32[4,4,128]{2,1,0:T(4,128)}) custom-call(bf16[256,512]{1,0:T(8,128)(2,1)} %tok_hbm.1, bf16[256,512]{1,0:T(8,128)(2,1)} %cot_hbm.1, bf16[4,128,128]{2,1,0:T(8,128)(2,1)} %up_one_hbm.1, bf16[4,416,128]{2,1,0:T(8,128)(2,1)} %bitcast.2, ...), custom_call_target="tpu_custom_call" | custom-call | tf_op jit(solution)/shard_map/pallas_call | solution.py:462
  65.3 1.7 %shard_map.102 = (bf16[256,512]{1,0:T(8,128)(2,1)}, f32[4,4,128]{2,1,0:T(4,128)}, f32[4,4,416]{2,1,0:T(4,128)}, f32[13,4,128]{2,1,0:T(4,128)}, f32[4,4,128]{2,1,0:T(4,128)}) custom-call(bf16[256,512]{1,0:T(8,128)(2,1)} %get-tuple-element.15.refs_0_, f32[4,4,128]{2,1,0:T(4,128)} %get-tuple-element.16.refs_1_, f32[4,4,416]{2,1,0:T(4,128)} %get-tuple-element.17.refs_2_, ...), custom_call_target="tpu_custom_call" | custom-call | tf_op jit(solution)/shard_map/pallas_call | solution.py:477
